TPU v7x, 32 devices: a whole 2x2x4 slice. The times are simulated.
32 devices in a mesh: gx: 4 (over z), gy: 2 (over y), gz: 4 (over x, core).
Axes of the slice: x: 2, y: 2, z: 4, core: 2. Of those that a mesh axis runs over, the one named last changes fastest.
Arguments:
- offsets: float32 [3, 8, 4, 8, 128], P(None, 'gx', 'gy', 'gz'), may hold values from 0 to 1
- features: bfloat16 [16, 8, 4, 8, 128], P(None, 'gx', 'gy', 'gz'), may hold values from -6 to 6
- charges: float32 [8, 8, 4, 8, 128], P(None, 'gx', 'gy', 'gz'), may hold values from -3 to 3
- counts: int32 [8, 4, 8], P('gx', 'gy', 'gz'), may hold values from 64 to 128, as said below
- waves: int32 [3, 2048], replicated, may hold values from -8 to 8, as said below
- kernel: float32 [8, 2048], replicated, may hold values from 0.1 to 3
- w_feat: float32 [16, 16], replicated, may hold values from -1.5 to 1.5
- w_charge_h: float32 [16, 8], replicated, may hold values from -1.5 to 1.5
- w_charge_f: float32 [8, 8], replicated, may hold values from -2 to 2
- charge_bias: float32 [8], replicated, may hold values from -1 to 1
- w_move_h: float32 [16, 3], replicated, may hold values from -1.5 to 1.5
- w_move_f: float32 [8, 3], replicated, may hold values from -2 to 2
Outputs:
- new_offsets: float32 [3, 8, 4, 8, 128], P(None, 'gx', 'gy', 'gz')
- new_charges: float32 [8, 8, 4, 8, 128], P(None, 'gx', 'gy', 'gz')
- new_features: bfloat16 [16, 8, 4, 8, 128], P(None, 'gx', 'gy', 'gz')
- last_field: float32 [8, 8, 4, 8, 128], P(None, 'gx', 'gy', 'gz')
Inputs may be any that keep to these rules, and one draw needn't show every extreme that they name: `counts`: live atoms of each cell; slots from the count on are empty and their entries are ignored. `waves`: the first component of every wavevector is from 1 to 8.
All inputs are finite; a program needn't handle non-finite values.
Results may differ from a plain program's by a relative error of at most 0.0042.
Values may be sent and summed in bfloat16 or wider, within the bound.
A program may use at most 64 MiB of HBM per device.

v0:
```python
import math

import jax
import jax.numpy as jnp
from jax import lax
from jax.sharding import PartitionSpec as P

STEPS = 2
ITERS = 2


RC_COEF = 1.0 / 0.72
STEP_LEN = 0.1
TWO_PI = 2.0 * math.pi
PRECISE = lax.Precision.HIGHEST


def extended(block, sides, width):
    for axis, dim in sides:
        count = lax.axis_size(axis)
        forward = [(i, i + 1) for i in range(count - 1)]
        forward.append((count - 1, 0))
        backward = [(target, source) for source, target in forward]
        low = lax.ppermute(
            lax.slice_in_dim(block, block.shape[dim] - width, None, axis=dim), axis, forward
        )
        high = lax.ppermute(lax.slice_in_dim(block, 0, width, axis=dim), axis, backward)
        block = jnp.concatenate([low, block, high], axis=dim)
    return block


def phase_table(frac_rows, wave_float):
    theta = TWO_PI * (
        wave_float[0][None, :] * frac_rows[0][:, None]
        + wave_float[1][None, :] * frac_rows[1][:, None]
        + wave_float[2][None, :] * frac_rows[2][:, None]
    )
    return jnp.concatenate([jnp.cos(theta), jnp.sin(theta)], axis=1)


def pair_messages(positions, feats, valid_slot):
    size_x, size_y, size_z = (valid_slot.shape[0], valid_slot.shape[1], valid_slot.shape[2])
    packed = jnp.concatenate([positions, valid_slot[None]], axis=0)
    rim_pos = extended(packed, (("gx", 1), ("gy", 2), ("gz", 3)), 1)
    rim_feat = extended(feats, (("gx", 1), ("gy", 2), ("gz", 3)), 1)
    message = jnp.zeros(feats.shape, jnp.float32)
    norm_sum = jnp.zeros(valid_slot.shape, jnp.float32)
    for shift_x in (-1, 0, 1):
        for shift_y in (-1, 0, 1):
            for shift_z in (-1, 0, 1):
                near_pos = rim_pos[
                    :,
                    1 + shift_x : 1 + shift_x + size_x,
                    1 + shift_y : 1 + shift_y + size_y,
                    1 + shift_z : 1 + shift_z + size_z,
                ]
                near_feat = rim_feat[
                    :,
                    1 + shift_x : 1 + shift_x + size_x,
                    1 + shift_y : 1 + shift_y + size_y,
                    1 + shift_z : 1 + shift_z + size_z,
                ]
                dist_x = near_pos[0][..., None, :] - positions[0][..., :, None] + shift_x
                dist_y = near_pos[1][..., None, :] - positions[1][..., :, None] + shift_y
                dist_z = near_pos[2][..., None, :] - positions[2][..., :, None] + shift_z
                dist_sq = dist_x * dist_x + dist_y * dist_y + dist_z * dist_z
                weight = (
                    valid_slot[..., :, None]
                    * near_pos[3][..., None, :]
                    * jnp.exp(-dist_sq * RC_COEF)
                ).astype(jnp.bfloat16)
                message = message + jnp.einsum(
                    "xyzab,cxyzb->cxyza", weight, near_feat, preferred_element_type=jnp.float32
                )
                norm_sum = norm_sum + jnp.sum(weight.astype(jnp.float32), axis=-1)
    return message / jnp.sqrt(jnp.maximum(norm_sum, 1.0))


def to_cells(grid_array):
    shape_now = grid_array.shape
    return grid_array.reshape(
        shape_now[0], shape_now[1] * shape_now[2] * shape_now[3], shape_now[4]
    ).transpose(1, 0, 2)


def from_cells(cell_array, grid_shape):
    return cell_array.transpose(1, 0, 2).reshape(
        cell_array.shape[1], grid_shape[0], grid_shape[1], grid_shape[2], grid_shape[3]
    )


def structure_local(frac_cells, charge_rows, wave_float):

    def structure_per_cell(running, item_pair):
        return (
            running
            + jnp.dot(item_pair[1], phase_table(item_pair[0], wave_float), precision=PRECISE),
            None,
        )

    start = jnp.zeros((charge_rows.shape[1], 2 * wave_float.shape[1]), jnp.float32)
    summed, _ = lax.scan(structure_per_cell, start, (frac_cells, charge_rows))
    return summed


def field_local(frac_cells, weighted, wave_float, scale):

    def field_per_cell(frac_rows):
        return jnp.dot(weighted, phase_table(frac_rows, wave_float).T, precision=PRECISE) * scale

    return lax.map(field_per_cell, frac_cells)


def charge_update(neutral, field_cells, hproj, valid_cells, w_charge_f, charge_bias):
    fproj = jnp.einsum("dc,ndp->ncp", w_charge_f, field_cells, precision=PRECISE)
    return valid_cells[:, None, :] * (
        0.5 * neutral + jnp.tanh(hproj + fproj + charge_bias[None, :, None])
    )


def on_device(
    offsets,
    features,
    charges,
    counts,
    waves,
    kernel,
    w_feat,
    w_charge_h,
    w_charge_f,
    charge_bias,
    w_move_h,
    w_move_f,
):
    size_x, size_y, size_z, capacity = (
        offsets.shape[1],
        offsets.shape[2],
        offsets.shape[3],
        offsets.shape[4],
    )
    grid_shape = (size_x, size_y, size_z, capacity)
    n_cells = size_x * size_y * size_z
    grid_x = size_x * lax.axis_size("gx")
    grid_y = size_y * lax.axis_size("gy")
    grid_z = size_z * lax.axis_size("gz")
    scale = 1.0 / math.sqrt(grid_x * grid_y * grid_z * capacity * waves.shape[1])
    wave_float = waves.astype(jnp.float32)
    doubled = jnp.concatenate([kernel, kernel], axis=1)
    valid_slot = (
        jnp.arange(capacity, dtype=jnp.int32)[None, None, None, :] < counts[..., None]
    ).astype(jnp.float32)
    valid_cells = valid_slot.reshape(n_cells, capacity)
    cell_x = (lax.axis_index("gx") * size_x + jnp.arange(size_x, dtype=jnp.int32)).astype(
        jnp.float32
    )
    cell_y = (lax.axis_index("gy") * size_y + jnp.arange(size_y, dtype=jnp.int32)).astype(
        jnp.float32
    )
    cell_z = (lax.axis_index("gz") * size_z + jnp.arange(size_z, dtype=jnp.int32)).astype(
        jnp.float32
    )
    positions = offsets
    feats = features
    charge_cells = to_cells(charges * valid_slot[None])
    field_cells = jnp.zeros_like(charge_cells)
    for step_index in range(STEPS):
        message = pair_messages(positions, feats, valid_slot)
        feats = (
            feats.astype(jnp.float32)
            + jnp.tanh(jnp.einsum("fg,fxyzp->gxyzp", w_feat, message, precision=PRECISE))
        ).astype(jnp.bfloat16)
        frac_x = (cell_x[:, None, None, None] + positions[0]) / grid_x
        frac_y = (cell_y[None, :, None, None] + positions[1]) / grid_y
        frac_z = (cell_z[None, None, :, None] + positions[2]) / grid_z
        frac_cells = to_cells(jnp.stack([frac_x, frac_y, frac_z]))
        hproj = jnp.einsum(
            "fc,nfp->ncp", w_charge_h, to_cells(feats.astype(jnp.float32)), precision=PRECISE
        )
        for sweep in range(ITERS):
            totals, atom_count = lax.psum(
                (jnp.sum(charge_cells, axis=(0, 2)), jnp.sum(valid_cells)), ("gx", "gy", "gz")
            )
            average = totals / atom_count
            neutral = valid_cells[:, None, :] * (charge_cells - average[None, :, None])
            local_rows = structure_local(frac_cells, neutral, wave_float)
            summed = lax.psum(local_rows, ("gx", "gy", "gz"))
            field_cells = field_local(frac_cells, doubled * summed, wave_float, scale)
            charge_cells = charge_update(
                neutral, field_cells, hproj, valid_cells, w_charge_f, charge_bias
            )
        field_grid = from_cells(field_cells, grid_shape)
        move = jnp.tanh(
            jnp.einsum("fd,fxyzp->dxyzp", w_move_h, message, precision=PRECISE)
            + jnp.einsum("cd,cxyzp->dxyzp", w_move_f, field_grid, precision=PRECISE)
        )
        positions = positions + STEP_LEN * valid_slot * move
    return (
        positions,
        from_cells(charge_cells, grid_shape),
        feats,
        from_cells(field_cells, grid_shape),
    )


def solution(mesh):
    in_specs = (
        P(None, "gx", "gy", "gz", None),
        P(None, "gx", "gy", "gz", None),
        P(None, "gx", "gy", "gz", None),
        P("gx", "gy", "gz"),
        P(),
        P(),
        P(),
        P(),
        P(),
        P(),
        P(),
        P(),
    )
    out_specs = (
        P(None, "gx", "gy", "gz", None),
        P(None, "gx", "gy", "gz", None),
        P(None, "gx", "gy", "gz", None),
        P(None, "gx", "gy", "gz", None),
    )
    return jax.shard_map(
        on_device, mesh=mesh, in_specs=in_specs, out_specs=out_specs, check_vma=False
    )
```

profile of v0, /device:TPU:0, one launch (start us, length us, event | category | flops | bytes accessed | tf_op | source)
XLA Modules:
  0.0 1063.2 jit_solution(9132719720172220629)
XLA Ops:
  23.2 38.3 %all-reduce = (f32[8]{0:T(128)S(1)}, f32[]{:T(128)}) all-reduce(f32[8]{0:T(128)S(1)} %get-tuple-element.440, f32[]{:T(128)} %fusion.264), channel_id=1, replica_groups=mesh['gx'=4,'gy'=2,'gz'=4] {'gx','gy','gz'}, use_global_device_ids=true, to_apply=%region_28.0 | all-reduce | flops 9 | bytes 72 | tf_op jit(solution)/shard_map/psum | solution.py:180
  62.3 41.4 %while.88 = (s32[]{:T(128)}, f32[8,4096]{1,0:T(8,128)S(1)}, f32[8,8,128]{2,1,0:T(8,128)S(1)}, f32[3,2048]{1,0:T(4,128)S(1)}, f32[8,3,128]{2,1,0:T(4,128)S(1)}, /*index=5*/s32[]{:T(128)}, s32[]{:T(128)}) while((s32[]{:T(128)}, f32[8,4096]{1,0:T(8,128)S(1)}, f32[8,8,128]{2,1,0:T(8,128)S(1)}, f32[3,2048]{1,0:T(4,128)S(1)}, ...), condition=%wide.region_32.33_spmd.clone, body=%wide.region_31.32_spmd.clone.sunk | while | flops 52494336 | bytes 4542047 | solution.py:102
  62.4 4.0 fusion.524
  67.6 4.0 fusion.524
  72.7 4.0 fusion.524
  77.9 4.0 fusion.524
  83.1 4.0 fusion.524
  88.2 4.0 fusion.524
  93.4 4.0 fusion.524
  98.6 4.0 fusion.524
  135.7 92.1 %all-reduce.6.cloned.1.call-done = f32[8,4096]{1,0:T(8,128)} async-done(((f32[8,4096]{1,0:T(8,128)}), f32[8,4096]{1,0:T(8,128)}) %all-reduce.6.cloned.1.call-update) | async-done | bytes 131088 | tf_op jit(solution)/shard_map/psum | solution.py:186
  228.8 46.6 %while.84 = (s32[]{:T(128)}, f32[8,8,128]{2,1,0:T(8,128)S(1)}, f32[3,2048]{1,0:T(4,128)S(1)}, f32[8,3,128]{2,1,0:T(4,128)S(1)}, f32[8,4096]{1,0:T(8,128)S(1)}, /*index=5*/s32[]{:T(128)}) while((s32[]{:T(128)}, f32[8,8,128]{2,1,0:T(8,128)S(1)}, f32[3,2048]{1,0:T(4,128)S(1)}, f32[8,3,128]{2,1,0:T(4,128)S(1)}, f32[8,4096]{1,0:T(8,128)S(1)}, ...), condition=%wide.region_35.36_spmd, body=%wide.region_34.35_spmd.sunk | while | flops 52429824 | bytes 4410957 | solution.py:111
  228.8 4.0 fusion.504
  234.6 4.0 fusion.504
  240.4 4.0 fusion.504
  246.2 4.0 fusion.504
  252.0 4.0 fusion.504
  257.7 4.0 fusion.504
  263.5 4.0 fusion.504
  269.3 4.0 fusion.504
  289.5 39.2 %psum.75 = f32[8]{0:T(128)S(1)} all-reduce(f32[8]{0:T(128)S(1)} %get-tuple-element.764), channel_id=1, replica_groups=mesh['gx'=4,'gy'=2,'gz'=4] {'gx','gy','gz'}, use_global_device_ids=true, to_apply=%region_37.38 | all-reduce | flops 8 | bytes 64 | tf_op jit(solution)/shard_map/psum | solution.py:180
  333.3 41.5 %while.89 = (s32[]{:T(128)}, f32[8,4096]{1,0:T(8,128)S(1)}, f32[8,8,128]{2,1,0:T(8,128)S(1)}, f32[3,2048]{1,0:T(4,128)S(1)}, f32[8,3,128]{2,1,0:T(4,128)S(1)}, /*index=5*/s32[]{:T(128)}, s32[]{:T(128)}) while((s32[]{:T(128)}, f32[8,4096]{1,0:T(8,128)S(1)}, f32[8,8,128]{2,1,0:T(8,128)S(1)}, f32[3,2048]{1,0:T(4,128)S(1)}, ...), condition=%wide.region_39.40_spmd.clone, body=%wide.region_38.39_spmd.clone.sunk | while | flops 52494336 | bytes 4542047 | solution.py:102
  333.5 4.0 fusion.528
  343.9 4.0 fusion.528
  349.0 4.0 fusion.528
  364.5 4.0 fusion.528
  369.7 4.0 fusion.528
  383.7 113.3 %all-reduce.8.cloned.1.call-done = f32[8,4096]{1,0:T(8,128)} async-done(((f32[8,4096]{1,0:T(8,128)}), f32[8,4096]{1,0:T(8,128)}) %all-reduce.8.cloned.1.call-update) | async-done | bytes 131088 | tf_op jit(solution)/shard_map/psum | solution.py:186
  497.9 46.2 %while.85 = (s32[]{:T(128)}, f32[8,8,128]{2,1,0:T(8,128)S(1)}, f32[3,2048]{1,0:T(4,128)S(1)}, f32[8,3,128]{2,1,0:T(4,128)S(1)}, f32[8,4096]{1,0:T(8,128)S(1)}, /*index=5*/s32[]{:T(128)}) while((s32[]{:T(128)}, f32[8,8,128]{2,1,0:T(8,128)S(1)}, f32[3,2048]{1,0:T(4,128)S(1)}, f32[8,3,128]{2,1,0:T(4,128)S(1)}, f32[8,4096]{1,0:T(8,128)S(1)}, ...), condition=%wide.region_42.43_spmd, body=%wide.region_41.42_spmd.sunk | while | flops 52429824 | bytes 4410957 | solution.py:111
  498.0 4.0 fusion.509
  509.5 4.0 fusion.509
  521.1 4.0 fusion.509
  526.9 4.0 fusion.509
  538.4 4.0 fusion.509
  544.5 39.4 %psum.77 = f32[8]{0:T(128)S(1)} all-reduce(f32[8]{0:T(128)S(1)} %get-tuple-element.766), channel_id=1, replica_groups=mesh['gx'=4,'gy'=2,'gz'=4] {'gx','gy','gz'}, use_global_device_ids=true, to_apply=%region_71.72 | all-reduce | flops 8 | bytes 64 | tf_op jit(solution)/shard_map/psum | solution.py:180
  588.6 41.3 %while.90 = (s32[]{:T(128)}, f32[8,4096]{1,0:T(8,128)S(1)}, f32[8,8,128]{2,1,0:T(8,128)S(1)}, f32[3,2048]{1,0:T(4,128)S(1)}, f32[8,3,128]{2,1,0:T(4,128)S(1)}, /*index=5*/s32[]{:T(128)}, s32[]{:T(128)}) while((s32[]{:T(128)}, f32[8,4096]{1,0:T(8,128)S(1)}, f32[8,8,128]{2,1,0:T(8,128)S(1)}, f32[3,2048]{1,0:T(4,128)S(1)}, ...), condition=%wide.region_73.74_spmd.clone, body=%wide.region_72.73_spmd.clone.sunk | while | flops 52494336 | bytes 4542047 | solution.py:102
  588.7 4.0 fusion.532
  593.8 4.0 fusion.532
  599.0 4.0 fusion.532
  604.2 4.0 fusion.532
  609.3 4.0 fusion.532
  614.5 4.0 fusion.532
  619.7 4.0 fusion.532
  624.8 4.0 fusion.532
  673.1 82.2 %all-reduce.10.cloned.1.call-done = f32[8,4096]{1,0:T(8,128)} async-done(((f32[8,4096]{1,0:T(8,128)}), f32[8,4096]{1,0:T(8,128)}) %all-reduce.10.cloned.1.call-update) | async-done | bytes 131088 | tf_op jit(solution)/shard_map/psum | solution.py:186
  756.3 46.2 %while.86 = (s32[]{:T(128)}, f32[8,8,128]{2,1,0:T(8,128)S(1)}, f32[3,2048]{1,0:T(4,128)S(1)}, f32[8,3,128]{2,1,0:T(4,128)S(1)}, f32[8,4096]{1,0:T(8,128)S(1)}, /*index=5*/s32[]{:T(128)}) while((s32[]{:T(128)}, f32[8,8,128]{2,1,0:T(8,128)S(1)}, f32[3,2048]{1,0:T(4,128)S(1)}, f32[8,3,128]{2,1,0:T(4,128)S(1)}, f32[8,4096]{1,0:T(8,128)S(1)}, ...), condition=%wide.region_76.77_spmd, body=%wide.region_75.76_spmd.sunk | while | flops 52429824 | bytes 4410957 | solution.py:111
  756.4 4.0 fusion.514
  767.9 4.0 fusion.514
  773.7 4.0 fusion.514
  785.3 4.0 fusion.514
  796.8 4.0 fusion.514
  802.9 39.4 %psum.79 = f32[8]{0:T(128)S(1)} all-reduce(f32[8]{0:T(128)S(1)} %get-tuple-element.768), channel_id=1, replica_groups=mesh['gx'=4,'gy'=2,'gz'=4] {'gx','gy','gz'}, use_global_device_ids=true, to_apply=%region_78.79 | all-reduce | flops 8 | bytes 64 | tf_op jit(solution)/shard_map/psum | solution.py:180
  843.1 41.3 %while.91 = (s32[]{:T(128)}, f32[8,4096]{1,0:T(8,128)S(1)}, f32[8,8,128]{2,1,0:T(8,128)S(1)}, f32[3,2048]{1,0:T(4,128)S(1)}, f32[8,3,128]{2,1,0:T(4,128)S(1)}, /*index=5*/s32[]{:T(128)}, s32[]{:T(128)}) while((s32[]{:T(128)}, f32[8,4096]{1,0:T(8,128)S(1)}, f32[8,8,128]{2,1,0:T(8,128)S(1)}, f32[3,2048]{1,0:T(4,128)S(1)}, ...), condition=%wide.region_80.81_spmd.clone, body=%wide.region_79.80_spmd.clone.sunk | while | flops 52494336 | bytes 4542047 | solution.py:102
  848.3 4.0 fusion.536
  853.5 4.0 fusion.536
  858.6 4.0 fusion.536
  874.1 4.0 fusion.536
  879.3 4.0 fusion.536
  885.9 121.7 %all-reduce.12.cloned.1.call-done = f32[8,4096]{1,0:T(8,128)} async-done(((f32[8,4096]{1,0:T(8,128)}), f32[8,4096]{1,0:T(8,128)}) %all-reduce.12.cloned.1.call-update) | async-done | bytes 131088 | tf_op jit(solution)/shard_map/psum | solution.py:186
  1008.5 46.3 %while.87 = (s32[]{:T(128)}, f32[8,8,128]{2,1,0:T(8,128)S(1)}, f32[3,2048]{1,0:T(4,128)S(1)}, f32[8,3,128]{2,1,0:T(4,128)S(1)}, f32[8,4096]{1,0:T(8,128)S(1)}, /*index=5*/s32[]{:T(128)}) while((s32[]{:T(128)}, f32[8,8,128]{2,1,0:T(8,128)S(1)}, f32[3,2048]{1,0:T(4,128)S(1)}, f32[8,3,128]{2,1,0:T(4,128)S(1)}, f32[8,4096]{1,0:T(8,128)S(1)}, ...), condition=%wide.region_83.84_spmd, body=%wide.region_82.83_spmd.sunk | while | flops 52429824 | bytes 4410957 | solution.py:111
  1008.5 4.0 fusion.519
  1037.5 4.0 fusion.519
  1043.2 4.0 fusion.519
  1049.0 4.0 fusion.519
  (529 shorter events, 288.1 us)
Async XLA Ops:
  7.2 281.5 %copy-start = (f32[16,16]{1,0:T(8,128)S(1)}, f32[16,16]{1,0:T(8,128)}, u32[]{:S(2)}) copy-start(f32[16,16]{1,0:T(8,128)} %param.34) | copy-start | bytes 3076
  7.2 220.7 %all-reduce.6.cloned.1.call-start = ((), (), s32[]{:S(2)}) async-start(), calls=%async_computation | async-start | bytes 262144 | tf_op jit(solution)/shard_map/psum | solution.py:186
  8.7 97.2 %collective-permute-start.5 = (f32[4,1,2,2,128]{4,3,2,1,0:T(2,128)S(1)}, f32[4,1,2,2,128]{4,3,2,1,0:T(2,128)S(1)}, u32[]{:S(2)}, u32[]{:S(2)}) collective-permute-start(f32[4,1,2,2,128]{4,3,2,1,0:T(2,128)S(1)} %get-tuple-element.762), channel_id=1, source_target_pairs={{0,8},{8,16},{16,24},{24,0},{1,9},{9,17},{17,25},{25,1},{2,10},{10... | collective-permute-start | bytes 24584 | tf_op jit(solution)/shard_map/ppermute | solution.py:24
  11.8 94.1 %collective-permute-start.6 = (f32[4,1,2,2,128]{4,3,2,1,0:T(2,128)S(1)}, f32[4,1,2,2,128]{4,3,2,1,0:T(2,128)S(1)}, u32[]{:S(2)}, u32[]{:S(2)}) collective-permute-start(f32[4,1,2,2,128]{4,3,2,1,0:T(2,128)S(1)} %get-tuple-element.763), channel_id=1, source_target_pairs={{8,0},{16,8},{24,16},{0,24},{9,1},{17,9},{25,17},{1,25},{10,2},{18... | collective-permute-start | bytes 24584 | tf_op jit(solution)/shard_map/ppermute | solution.py:27
  14.6 94.0 %collective-permute-start = (bf16[16,1,2,2,128]{4,0,3,2,1:T(8,128)(2,1)S(1)}, bf16[16,1,2,2,128]{4,0,3,2,1:T(8,128)(2,1)S(1)}, u32[]{:S(2)}, u32[]{:S(2)}) collective-permute-start(bf16[16,1,2,2,128]{4,0,3,2,1:T(8,128)(2,1)S(1)} %get-tuple-element.725), channel_id=1, source_target_pairs={{0,8},{8,16},{16,24},{24,0},{1,9},{9,17},{17,25},{25,1},{2,10},{10... | collective-permute-start | bytes 49160 | tf_op jit(solution)/shard_map/ppermute | solution.py:24
  14.7 93.9 %collective-permute-start.1 = (bf16[16,1,2,2,128]{4,0,3,2,1:T(8,128)(2,1)S(1)}, bf16[16,1,2,2,128]{4,0,3,2,1:T(8,128)(2,1)S(1)}, u32[]{:S(2)}, u32[]{:S(2)}) collective-permute-start(bf16[16,1,2,2,128]{4,0,3,2,1:T(8,128)(2,1)S(1)} %get-tuple-element.724), channel_id=1, source_target_pairs={{8,0},{16,8},{24,16},{0,24},{9,1},{17,9},{25,17},{1,25},{10,2},{18... | collective-permute-start | bytes 49160 | tf_op jit(solution)/shard_map/ppermute | solution.py:27
  62.3 42.1 %copy-start.7 = (f32[8,2048]{1,0:T(8,128)S(1)}, f32[8,2048]{1,0:T(8,128)}, u32[]{:S(2)}) copy-start(f32[8,2048]{1,0:T(8,128)} %param.33) | copy-start | bytes 196612
  62.3 42.2 %copy-start.6 = (bf16[16,2,2,2,128]{4,3,2,1,0:T(2,128)(2,1)S(1)}, bf16[16,2,2,2,128]{4,3,2,1,0:T(2,128)(2,1)}, u32[]{:S(2)}) copy-start(bf16[16,2,2,2,128]{4,3,2,1,0:T(2,128)(2,1)} %param.29) | copy-start | bytes 98308
  103.7 0.7 copy-start.4
  104.4 392.6 %all-reduce.8.cloned.1.call-start = ((), (), s32[]{:S(2)}) async-start(), calls=%async_computation.1 | async-start | bytes 262144 | tf_op jit(solution)/shard_map/psum | solution.py:186
  104.4 1.4 copy-start.10
  104.5 1.4 copy-start.5
  106.0 7.4 collective-permute-start.7
  108.5 4.9 collective-permute-start.8
  108.7 7.2 collective-permute-start.2
  110.7 5.2 collective-permute-start.3
  113.4 9.8 collective-permute-start.11
  113.5 9.7 collective-permute-start.9
  116.0 159.5 %collective-permute-start.10 = (bf16[16,4,4,1,128]{4,0,3,2,1:T(8,128)(2,1)S(1)}, bf16[16,4,4,1,128]{4,0,3,2,1:T(8,128)(2,1)S(1)}, u32[]{:S(2)}, u32[]{:S(2)}) collective-permute-start(bf16[16,4,4,1,128]{4,0,3,2,1:T(8,128)(2,1)S(1)} %get-tuple-element.583), channel_id=1, source_target_pairs={{1,0},{2,1},{3,2},{0,3},{5,4},{6,5},{7,6},{4,7},{9,8},{10,9},{11,1... | collective-permute-start | bytes 196616 | tf_op jit(solution)/shard_map/ppermute | solution.py:27
  117.4 159.5 %collective-permute-start.4 = (bf16[16,4,4,1,128]{4,0,3,2,1:T(8,128)(2,1)S(1)}, bf16[16,4,4,1,128]{4,0,3,2,1:T(8,128)(2,1)S(1)}, u32[]{:S(2)}, u32[]{:S(2)}) collective-permute-start(bf16[16,4,4,1,128]{4,0,3,2,1:T(8,128)(2,1)S(1)} %get-tuple-element.582), channel_id=1, source_target_pairs={{0,1},{1,2},{2,3},{3,0},{4,5},{5,6},{6,7},{7,4},{8,9},{9,10},{10,1... | collective-permute-start | bytes 196616 | tf_op jit(solution)/shard_map/ppermute | solution.py:24
  287.9 1.1 copy-start.11
  287.9 1.2 copy-start.9
  287.9 1.2 copy-start.14
  329.3 46.2 %collective-permute-start.12 = (bf16[16,1,2,2,128]{4,0,3,2,1:T(8,128)(2,1)S(1)}, bf16[16,1,2,2,128]{4,0,3,2,1:T(8,128)(2,1)S(1)}, u32[]{:S(2)}, u32[]{:S(2)}) collective-permute-start(bf16[16,1,2,2,128]{4,0,3,2,1:T(8,128)(2,1)S(1)} %get-tuple-element.720), channel_id=1, source_target_pairs={{0,8},{8,16},{16,24},{24,0},{1,9},{9,17},{17,25},{25,1},{2,10},{10... | collective-permute-start | bytes 49160 | tf_op jit(solution)/shard_map/ppermute | solution.py:24
  330.8 44.8 %collective-permute-start.13 = (bf16[16,1,2,2,128]{4,0,3,2,1:T(8,128)(2,1)S(1)}, bf16[16,1,2,2,128]{4,0,3,2,1:T(8,128)(2,1)S(1)}, u32[]{:S(2)}, u32[]{:S(2)}) collective-permute-start(bf16[16,1,2,2,128]{4,0,3,2,1:T(8,128)(2,1)S(1)} %get-tuple-element.721), channel_id=1, source_target_pairs={{8,0},{16,8},{24,16},{0,24},{9,1},{17,9},{25,17},{1,25},{10,2},{18... | collective-permute-start | bytes 49160 | tf_op jit(solution)/shard_map/ppermute | solution.py:27
  333.3 44.7 %copy-start.13 = (f32[16,3]{0,1:T(4,128)S(1)}, f32[16,3]{0,1:T(4,128)}, u32[]{:S(2)}) copy-start(f32[16,3]{0,1:T(4,128)} %param.38) | copy-start | bytes 580
  374.8 0.7 copy-start.3
  375.5 379.9 %all-reduce.10.cloned.1.call-start = ((), (), s32[]{:S(2)}) async-start(), calls=%async_computation.2 | async-start | bytes 262144 | tf_op jit(solution)/shard_map/psum | solution.py:186
  375.6 4.2 collective-permute-start.14
  377.9 3.9 collective-permute-start.15
  381.9 264.9 %collective-permute-start.16 = (bf16[16,4,4,1,128]{4,0,3,2,1:T(8,128)(2,1)S(1)}, bf16[16,4,4,1,128]{4,0,3,2,1:T(8,128)(2,1)S(1)}, u32[]{:S(2)}, u32[]{:S(2)}) collective-permute-start(bf16[16,4,4,1,128]{4,0,3,2,1:T(8,128)(2,1)S(1)} %get-tuple-element.508), channel_id=1, source_target_pairs={{0,1},{1,2},{2,3},{3,0},{4,5},{5,6},{6,7},{7,4},{8,9},{9,10},{10,1... | collective-permute-start | bytes 196616 | tf_op jit(solution)/shard_map/ppermute | solution.py:24
  382.0 264.8 %collective-permute-start.22 = (bf16[16,4,4,1,128]{4,0,3,2,1:T(8,128)(2,1)S(1)}, bf16[16,4,4,1,128]{4,0,3,2,1:T(8,128)(2,1)S(1)}, u32[]{:S(2)}, u32[]{:S(2)}) collective-permute-start(bf16[16,4,4,1,128]{4,0,3,2,1:T(8,128)(2,1)S(1)} %get-tuple-element.509), channel_id=1, source_target_pairs={{1,0},{2,1},{3,2},{0,3},{5,4},{6,5},{7,6},{4,7},{9,8},{10,9},{11,1... | collective-permute-start | bytes 196616 | tf_op jit(solution)/shard_map/ppermute | solution.py:27
  497.9 86.7 %copy-start.12 = (f32[8,3]{0,1:T(4,128)S(1)}, f32[8,3]{0,1:T(4,128)}, u32[]{:S(2)}) copy-start(f32[8,3]{0,1:T(4,128)} %param.39) | copy-start | bytes 292
  584.8 3.7 collective-permute-start.18
  587.1 43.5 %collective-permute-start.17 = (f32[4,1,2,2,128]{4,0,3,2,1:T(4,128)S(1)}, f32[4,1,2,2,128]{4,0,3,2,1:T(4,128)S(1)}, u32[]{:S(2)}, u32[]{:S(2)}) collective-permute-start(f32[4,1,2,2,128]{4,0,3,2,1:T(4,128)S(1)} %get-tuple-element.744), channel_id=1, source_target_pairs={{0,8},{8,16},{16,24},{24,0},{1,9},{9,17},{17,25},{25,1},{2,10},{10... | collective-permute-start | bytes 24584 | tf_op jit(solution)/shard_map/ppermute | solution.py:24
  629.9 0.7 copy-start.2
  630.6 376.9 %all-reduce.12.cloned.1.call-start = ((), (), s32[]{:S(2)}) async-start(), calls=%async_computation.3 | async-start | bytes 262144 | tf_op jit(solution)/shard_map/psum | solution.py:186
  630.7 6.3 collective-permute-start.19
  633.1 4.0 collective-permute-start.20
  637.1 9.7 collective-permute-start.21
  637.2 9.7 collective-permute-start.23
  884.4 0.7 copy-start.1
  1055.7 0.8 copy-start.8
Sparse Core Ops, SparseCore 0:
  104.5 123.3 all-reduce.5
  375.6 121.2 all-reduce.7
  630.7 124.5 all-reduce.9
  885.2 122.3 all-reduce.11
where the time goes:
time: 1070 us; the launch traced here: 1060 us
  waiting for transfers between devices  414 us (39%)
  other arithmetic  296 us (28%)
  blocking collectives  156 us (15%)
  matrix products  138 us (13%)
  starting transfers between devices  30.8 us (3%)
  between operations  14.9 us (1%)
    psum x4, waiting for transfers between devices, on_device(): summed = lax.psum(local_rows, ('gx', 'gy', 'gz'))  409 us
    cos x64, other arithmetic, phase_table(): return jnp.concatenate([jnp.cos(theta), jnp.sin(theta)], axis=1)  256 us
    psum x4, blocking collectives, on_device(): lax.psum((jnp.sum(charge_cells, axis=(0, 2)), jnp.sum(valid_cells)), ('gx...  156 us
    dot_general x32, matrix products, field_per_cell(): jnp.dot(weighted, phase_table(frac_rows, wave_float).T, precision=PRECISE)  55.3 us
    dot_general x54, matrix products, pair_messages(): jnp.einsum('xyzab,cxyzb->cxyza', weight, near_feat, preferred_element_typ...  45.1 us
    dot_general x32, matrix products, structure_per_cell(): jnp.dot(item_pair[1], phase_table(item_pair[0], wave_float), precision=PR...  35 us
    reduce_sum x18, other arithmetic, pair_messages(): norm_sum = norm_sum + jnp.sum(weight.astype(jnp.float32), axis=-1)  28.6 us
  transfers between devices with their start and end apart: 28, of which 7 were waited for; matrix products, arithmetic and copies ran while one was open for 27% of the time, Pallas kernels for 0%

commit v1 on v0

v1 whole, which is shorter than its diff:
```python
import functools
import math

import jax
import jax.numpy as jnp
import numpy as np
from jax import lax
from jax.experimental import pallas as pl
from jax.experimental.pallas import tpu as pltpu
from jax.sharding import PartitionSpec as P

STEPS = 2
ITERS = 2
STEP_LEN = 0.1
CAP = 128
EXP_COEF = math.log2(math.e) / 0.72
FAR = 1.0e6
HI = lax.Precision.HIGHEST
MESH = pl.DeviceIdType.MESH
REC = 32
N_P = 37
TILES_PV = 5
TOT = 37
PV0 = 38
TILES = PV0 + TILES_PV


def fit(fn):
    cheb = np.polynomial.chebyshev.Chebyshev.interpolate(fn, 8, domain=[0.0, 0.25])
    return [float(v) for v in cheb.convert(kind=np.polynomial.Polynomial).coef]


COS_POLY = fit(lambda s: np.cos(2 * np.pi * np.sqrt(np.abs(s))))
SIN_POLY = fit(lambda s: 2 * np.pi * np.sinc(2 * np.sqrt(np.abs(s))))


def horner(coefs, x):
    total = jnp.full_like(x, coefs[-1])
    for c in reversed(coefs[:-1]):
        total = total * x + c
    return total


def split3(x):
    hi = x.astype(jnp.bfloat16)
    rest = x - hi.astype(jnp.float32)
    mid = rest.astype(jnp.bfloat16)
    low = (rest - mid.astype(jnp.float32)).astype(jnp.bfloat16)
    return hi, mid, low


def split2(x):
    hi = x.astype(jnp.bfloat16)
    return hi, (x - hi.astype(jnp.float32)).astype(jnp.bfloat16)


def dot(a, b, dims, precision=None):
    return lax.dot_general(
        a, b, (dims, ((), ())), precision=precision, preferred_element_type=jnp.float32
    )


def dot3(a, b, dims):
    ah, al = split2(a)
    bh, bl = split2(b)
    return dot(ah, bh, dims) + (dot(ah, bl, dims) + dot(al, bh, dims))


NN = ((1,), (0,))
NT = ((1,), (1,))
TN = ((0,), (0,))


def spans(size, d):
    if d == 0:
        return 1, 1, size
    if d > 0:
        return size, 0, 1
    return 1, size + 1, 1


def kernel_body(
    sizes, block, chunk,
    pos_in, feat_in, charge_in, valid_in, waves_ref, kern_ref, wfeat_ref, wch_ref, wcf_ref,
    bias_ref, wmh_ref, wmf_ref,
    pos_out, charge_out, feat_out, field_out,
    halo, bt_ref, a_ref, msg_ref, yz_ref, w_ref, payload, rs_buf, part_buf, gx_buf, full,
    halo_send, halo_recv, rs_send, rs_recv, gx_send, gx_recv, ag_send, ag_recv,
):
    nx, ny, nz = sizes
    sx, sy, sz = block
    atoms = sx * sy * sz * CAP
    plane = ny * nz
    mx, my, mz = lax.axis_index("gx"), lax.axis_index("gy"), lax.axis_index("gz")
    mp = my * nz + mz
    scale = 1.0 / math.sqrt(nx * sx * ny * sy * nz * sz * CAP * waves_ref.shape[1])

    def plane_id(d):
        p = lax.rem(mp + d, plane)
        return (mx, lax.div(p, nz), lax.rem(p, nz)), p

    barrier = pltpu.get_barrier_semaphore()
    for ddx in range(nx):
        for d in range(plane):
            if ddx == 0 and d == 0:
                continue
            (_, py, pz), _ = plane_id(d)
            pl.semaphore_signal(
                barrier, inc=1, device_id=(lax.rem(mx + ddx, nx), py, pz), device_id_type=MESH
            )

    valid = valid_in[...]
    cell = lax.broadcasted_iota(jnp.int32, (1, atoms), 1) // CAP
    loc = [cell // (sy * sz), (cell // sz) % sy, cell % sz]
    mine = [mx, my, mz]
    side = [nx * sx, ny * sy, nz * sz]
    cell_f = [
        (loc[j] + mine[j] * block[j]).astype(jnp.float32) for j in range(3)
    ]
    local_f = jnp.concatenate([v.astype(jnp.float32) for v in loc], axis=0) - 1.0
    lane = lax.broadcasted_iota(jnp.int32, (8, 128), 1)
    sub = lax.broadcasted_iota(jnp.int32, (8, 128), 0)
    k8 = (lax.broadcasted_iota(jnp.int32, (8, 1), 0) + 1).astype(jnp.float32)

    wy, wz = waves_ref[1:2, :], waves_ref[2:3, :]
    sgy = jnp.where(wy > 0, 1.0, 0.0) - jnp.where(wy < 0, 1.0, 0.0)
    sgz = jnp.where(wz > 0, 1.0, 0.0) - jnp.where(wz < 0, 1.0, 0.0)
    k8i = lax.broadcasted_iota(jnp.int32, (8, 1), 0) + 1
    oz = (jnp.abs(wz) == k8i).astype(jnp.float32)
    oy = (jnp.abs(wy) == k8i).astype(jnp.float32)
    oz0 = (wz == 0).astype(jnp.float32)
    oy0 = (wy == 0).astype(jnp.float32)
    hot = [oy[i : i + 1] * oz for i in range(8)] + [oy0 * oz, oy * oz0, oy0 * oz0 * (k8 == 1.0)]
    kern = kern_ref[...]
    lanes_k = [jnp.where(waves_ref[0:1, :] == i + 1, kern, 0.0) for i in range(8)]
    lanes_k = jnp.concatenate(lanes_k + lanes_k, axis=0)
    kh, kl = split2(lanes_k)
    sx_lane = jnp.where(lane >= 64, 1.0, -1.0)
    hot = jnp.concatenate(hot, axis=0)
    for i, sg in enumerate((None, sgy * sgz, sgy, sgz)):
        oh = (hot if sg is None else hot * sg).astype(jnp.bfloat16)
        w = (dot(oh, kh, NT) + dot(oh, kl, NT)) * scale
        if i >= 2:
            w = w * sx_lane[0:1]
        w_ref[i] = w

    pl.semaphore_wait(barrier, nx * plane - 1)

    def send_halo(step, pos, feats):
        hi, mid, low = split3(pos)
        rec = jnp.concatenate(
            [feats.astype(jnp.float32)]
            + [v.astype(jnp.float32) for v in (hi, mid, low)]
            + [valid, jnp.zeros((REC - 26, atoms), jnp.float32)],
            axis=0,
        ).astype(jnp.bfloat16)
        for x in range(sx):
            for y in range(sy):
                for z in range(sz):
                    n = (x * sy + y) * sz + z
                    halo[step, 1 + x, 1 + y, 1 + z] = rec[:, n * CAP : (n + 1) * CAP]
        copies = []
        for dx in (-1, 0, 1):
            for dy in (-1, 0, 1):
                for dz in (-1, 0, 1):
                    if dx == dy == dz == 0:
                        continue
                    n = len(copies)
                    x, y, z = spans(sx, dx), spans(sy, dy), spans(sz, dz)
                    copy = pltpu.make_async_remote_copy(
                        src_ref=halo.at[
                            step, pl.ds(x[0], x[2]), pl.ds(y[0], y[2]), pl.ds(z[0], z[2])
                        ],
                        dst_ref=halo.at[
                            step, pl.ds(x[1], x[2]), pl.ds(y[1], y[2]), pl.ds(z[1], z[2])
                        ],
                        send_sem=halo_send.at[step, n],
                        recv_sem=halo_recv.at[step, n],
                        device_id=(
                            lax.rem(mx + nx + dx, nx),
                            lax.rem(my + ny + dy, ny),
                            lax.rem(mz + nz + dz, nz),
                        ),
                        device_id_type=MESH,
                    )
                    copy.start()
                    copies.append(copy)
        return copies

    def pair_rows(p, ok, own):
        width = p.shape[1]
        sq = -EXP_COEF * (p[0:1] * p[0:1] + p[1:2] * p[1:2] + p[2:3] * p[2:3])
        one = jnp.ones((3, width), jnp.float32)
        f32 = lambda parts: [v.astype(jnp.float32) for v in parts]
        if own:
            hi, mid, low = f32(split3(p * (2.0 * EXP_COEF)))
            rows = [hi, mid, low, hi, mid, hi, one] + f32(split3(sq))
        else:
            hi, mid, low = f32(split3(p))
            rows = [hi, hi, hi, mid, mid, low] + f32(split3(sq - FAR * (1.0 - ok))) + [one]
        return jnp.concatenate(rows + [jnp.zeros((8, width), jnp.float32)], axis=0)

    def pair_messages(step, pos):
        own = pair_rows(pos + local_f, None, True).astype(jnp.bfloat16)
        for i in range(sx * sy):
            a_ref[i] = own[:, i * sz * CAP : (i + 1) * sz * CAP]
        wide = (sz + 2) * CAP
        zrow = (lax.broadcasted_iota(jnp.int32, (1, wide), 1) // CAP).astype(jnp.float32) - 2.0

        def prepare(g, carry):
            gx_i, gy_i = lax.div(g, sy + 2), lax.rem(g, sy + 2)
            rec = jnp.concatenate(
                [halo[step, gx_i, gy_i, z] for z in range(sz + 2)], axis=1
            ).astype(jnp.float32)
            p = rec[16:19] + rec[19:22] + rec[22:25]
            ones = jnp.ones((1, wide), jnp.float32)
            base = jnp.concatenate(
                [
                    ones * (gx_i.astype(jnp.float32) - 2.0),
                    ones * (gy_i.astype(jnp.float32) - 2.0),
                    zrow,
                ],
                axis=0,
            )
            bt_ref[g] = jnp.transpose(pair_rows(p + base, rec[25:26], False)).astype(jnp.bfloat16)
            return carry

        lax.fori_loop(0, (sx + 2) * (sy + 2), prepare, 0)

        def per_column(i, carry):
            x, y = lax.div(i, sy), lax.rem(i, sy)
            for z in range(sz):
                mine_a = a_ref[i, :, z * CAP : (z + 1) * CAP]
                total = jnp.zeros((REC, CAP), jnp.float32)
                for dx in range(3):
                    for dy in range(3):
                        g = (x + dx) * (sy + 2) + y + dy
                        rows = bt_ref[g, z * CAP : (z + 3) * CAP, :]
                        weight = jnp.exp2(dot(rows, mine_a, NN)).astype(jnp.bfloat16)
                        rec = jnp.concatenate(
                            [halo[step, x + dx, y + dy, z + k] for k in range(3)], axis=1
                        )
                        total = total + dot(rec, weight, NN)
                msg_ref[i, :, z * CAP : (z + 1) * CAP] = total
            return carry

        lax.fori_loop(0, sx * sy, per_column, 0)
        total = jnp.concatenate([msg_ref[i] for i in range(sx * sy)], axis=1) * valid
        return total[0:16] / jnp.sqrt(jnp.maximum(total[25:26], 1.0))

    def all_sum(r):
        copies = []
        for d in range(1, plane):
            device, p = plane_id(d)
            copy = pltpu.make_async_remote_copy(
                src_ref=payload.at[r, pl.ds(pl.multiple_of(p * chunk, 8), chunk)],
                dst_ref=rs_buf.at[r, d],
                send_sem=rs_send.at[r, d],
                recv_sem=rs_recv.at[r, d],
                device_id=device,
                device_id_type=MESH,
            )
            copy.start()
            copies.append(copy)
        total = payload[r, pl.ds(pl.multiple_of(mp * chunk, 8), chunk)]
        for d in range(1, plane):
            copies[d - 1].wait_recv()
            total = total + rs_buf[r, d]
        part_buf[r, 0] = total
        copies_x = []
        for d in range(1, nx):
            copy = pltpu.make_async_remote_copy(
                src_ref=part_buf.at[r, 0],
                dst_ref=gx_buf.at[r, d],
                send_sem=gx_send.at[r, d],
                recv_sem=gx_recv.at[r, d],
                device_id=(lax.rem(mx + d, nx), my, mz),
                device_id_type=MESH,
            )
            copy.start()
            copies_x.append(copy)
        for d in range(1, nx):
            copies_x[d - 1].wait_recv()
            total = total + gx_buf[r, d]
        here = pl.ds(pl.multiple_of(mp * chunk, 8), chunk)
        full[r, here] = total
        copies_g = []
        for d in range(1, plane):
            device, _ = plane_id(d)
            copy = pltpu.make_async_remote_copy(
                src_ref=full.at[r, here],
                dst_ref=full.at[r, here],
                send_sem=ag_send.at[r, d],
                recv_sem=ag_recv.at[r, d],
                device_id=device,
                device_id_type=MESH,
            )
            copy.start()
            copies_g.append(copy)
        for copy in copies_g:
            copy.wait_recv()
        for copy in copies + copies_x + copies_g:
            copy.wait_send()

    def trig(pos):
        out = []
        for j in range(3):
            u = (cell_f[j] + pos[j : j + 1]) / float(side[j])
            t = k8 * u
            t = t - jnp.floor(t + 0.5)
            s = t * t
            out.append((horner(COS_POLY, s), t * horner(SIN_POLY, s)))
        return out

    block_ones = (
        lax.broadcasted_iota(jnp.int32, (128, 128), 0) // 8
        == lax.broadcasted_iota(jnp.int32, (128, 128), 1) // 8
    ).astype(jnp.bfloat16)

    pos = pos_in[...]
    feats = feat_in[...]
    charge = charge_in[...] * valid
    field = None
    count_row = jnp.zeros((1, 128), jnp.float32) + jnp.sum(valid, axis=1, keepdims=True)
    ones8 = jnp.ones((8, atoms), jnp.bfloat16)
    for step in range(STEPS):
        copies = send_halo(step, pos, feats)
        (cx, sxn), (cy, syn), (cz, szn) = trig(pos)
        xs = [v[i : i + 1] for v in (cx, sxn) for i in range(8)]
        zz = jnp.concatenate([cz, szn], axis=0)
        for i in range(16):
            yrow = (cy, syn)[i // 8][i % 8 : i % 8 + 1]
            yz_ref[i * 16 : (i + 1) * 16, :] = yrow * zz
        yz_ref[256:272, :] = zz
        yz_ref[272:288, :] = jnp.concatenate([cy, syn], axis=0)
        yz_ref[288:296, :] = jnp.where(k8 == 1.0, 1.0, 0.0) * jnp.ones((8, atoms), jnp.float32)
        yz = yz_ref[...]
        yh, yl = split2(yz)
        valid8 = jnp.ones((8, 1), jnp.float32) * valid
        xv = jnp.concatenate([x * valid8 for x in xs], axis=0)
        vh, vl = split2(xv)
        pv = dot(yh, vh, NT) + (dot(yh, vl, NT) + dot(yl, vh, NT))
        for t in range(TILES_PV):
            packed = jnp.zeros((8, 128), jnp.float32)
            for g in range(8):
                if t * 8 + g < N_P:
                    n = t * 8 + g
                    packed = jnp.where(lane % 8 == g, pv[n * 8 : n * 8 + 8], packed)
            payload[step * ITERS, (PV0 + t) * 8 : (PV0 + t + 1) * 8] = packed
        for copy in copies:
            copy.wait()
        message = pair_messages(step, pos)
        feats = (
            feats.astype(jnp.float32)
            + jnp.tanh(dot(wfeat_ref[...], message, TN, HI))
        ).astype(jnp.bfloat16)
        hproj = dot(wch_ref[...], feats.astype(jnp.float32), TN, HI) + bias_ref[...]
        for sweep in range(ITERS):
            r = step * ITERS + sweep
            qx = jnp.concatenate([x * charge for x in xs], axis=0)
            qh, ql = split2(qx)
            payload[r, 0 : N_P * 8] = dot(yh, qh, NT) + (dot(yh, ql, NT) + dot(yl, qh, NT))
            qrep = jnp.concatenate([charge] * 16, axis=0)
            th, tm, tl = split3(qrep)
            totals = dot(ones8, th, NT) + dot(ones8, tm, NT) + dot(ones8, tl, NT)
            payload[r, TOT * 8 : TOT * 8 + 8] = jnp.where(sub == 0, totals, count_row)
            if sweep > 0:
                payload[r, PV0 * 8 : TILES * 8] = jnp.zeros((TILES_PV * 8, 128), jnp.float32)
            if payload.shape[1] > TILES * 8:
                payload[r, TILES * 8 :] = jnp.zeros(
                    (payload.shape[1] - TILES * 8, 128), jnp.float32
                )
            all_sum(r)
            if sweep == 0:
                spread = []
                for n in range(N_P):
                    packed = full[r, (PV0 + n // 8) * 8 : (PV0 + n // 8) * 8 + 8]
                    spread.append(jnp.where(lane % 8 == n % 8, packed, 0.0))
                sh, sm, sl = split3(jnp.concatenate(spread, axis=0))
                pv_all = dot(sh, block_ones, NN) + dot(sm, block_ones, NN) + dot(sl, block_ones, NN)
            tot = full[r, TOT * 8 : TOT * 8 + 8]
            mean_row = tot[0:1] / tot[1:2]
            mean_col = jnp.sum(
                jnp.where(lane == sub, jnp.broadcast_to(mean_row, (8, 128)), 0.0),
                axis=1, keepdims=True,
            )
            neutral = valid * (charge - mean_col)
            p_all = full[r, 0 : N_P * 8] - mean_row * pv_all
            p_roll = pltpu.roll(p_all, 64, 1)
            tile = lambda a, n: a[n * 8 : n * 8 + 8]
            t_rows = []
            for yr in range(2):
                for ky in range(8):
                    for zr in range(2):
                        w = [w_ref[i, ky * 8 : ky * 8 + 8] for i in range(4)]
                        at = lambda a, b: ((a * 8 + ky) * 2 + b)
                        s_y, s_z = 2.0 * yr - 1.0, 2.0 * zr - 1.0
                        t_rows.append(
                            w[0] * tile(p_all, at(yr, zr))
                            - (s_y * s_z) * w[1] * tile(p_all, at(1 - yr, 1 - zr))
                            - s_y * w[2] * tile(p_roll, at(1 - yr, zr))
                            - s_z * w[3] * tile(p_roll, at(yr, 1 - zr))
                        )
            for zr in range(2):
                t_rows.append(
                    w_ref[0, 64:72] * tile(p_all, 32 + zr)
                    - (2.0 * zr - 1.0) * w_ref[3, 64:72] * tile(p_roll, 32 + 1 - zr)
                )
            for yr in range(2):
                t_rows.append(
                    w_ref[0, 72:80] * tile(p_all, 34 + yr)
                    - (2.0 * yr - 1.0) * w_ref[2, 72:80] * tile(p_roll, 34 + 1 - yr)
                )
            t_rows.append(w_ref[0, 80:88] * tile(p_all, 36))
            t_all = jnp.transpose(jnp.concatenate(t_rows, axis=0))
            fh, fl = split2(t_all)
            f_all = dot(fh, yh, NN) + (dot(fh, yl, NN) + dot(fl, yh, NN))
            field = xs[0] * f_all[0:8]
            for i in range(1, 16):
                field = field + xs[i] * f_all[i * 8 : i * 8 + 8]
            fproj = dot(wcf_ref[...], field, TN, HI)
            charge = valid * (0.5 * neutral + jnp.tanh(hproj + fproj))
        move = jnp.tanh(
            dot(wmh_ref[...], message, TN, HI) + dot(wmf_ref[...], field, TN, HI)
        )
        pos = pos + STEP_LEN * valid * move
    pos_out[...] = pos
    charge_out[...] = charge
    feat_out[...] = feats
    field_out[...] = field


def on_device(
    sizes, offsets, features, charges, counts, waves, kernel,
    w_feat, w_charge_h, w_charge_f, charge_bias, w_move_h, w_move_f,
):
    nx, ny, nz = sizes
    block = offsets.shape[1:4]
    sx, sy, sz = block
    atoms = sx * sy * sz * CAP
    plane = ny * nz
    chunk = -(-TILES // plane) * 8
    rounds = STEPS * ITERS
    valid = (jnp.arange(CAP, dtype=jnp.int32) < counts[..., None]).astype(jnp.float32)
    args = (
        offsets.reshape(3, atoms), features.reshape(16, atoms), charges.reshape(8, atoms),
        valid.reshape(1, atoms), waves, kernel, w_feat, w_charge_h, w_charge_f,
        charge_bias.reshape(8, 1), w_move_h, w_move_f,
    )
    vmem = pl.BlockSpec(memory_space=pltpu.VMEM)
    dma = pltpu.SemaphoreType.DMA
    outs = pl.pallas_call(
        functools.partial(kernel_body, sizes, block, chunk),
        out_shape=(
            jax.ShapeDtypeStruct((3, atoms), jnp.float32),
            jax.ShapeDtypeStruct((8, atoms), jnp.float32),
            jax.ShapeDtypeStruct((16, atoms), jnp.bfloat16),
            jax.ShapeDtypeStruct((8, atoms), jnp.float32),
        ),
        in_specs=[vmem] * len(args),
        out_specs=(vmem,) * 4,
        scratch_shapes=[
            pltpu.VMEM((STEPS, sx + 2, sy + 2, sz + 2, REC, CAP), jnp.bfloat16),
            pltpu.VMEM(((sx + 2) * (sy + 2), (sz + 2) * CAP, 32), jnp.bfloat16),
            pltpu.VMEM((sx * sy, 32, sz * CAP), jnp.bfloat16),
            pltpu.VMEM((sx * sy, REC, sz * CAP), jnp.float32),
            pltpu.VMEM((N_P * 8, atoms), jnp.float32),
            pltpu.VMEM((4, 88, 128), jnp.float32),
            pltpu.VMEM((rounds, plane * chunk, 128), jnp.float32),
            pltpu.VMEM((rounds, plane, chunk, 128), jnp.float32),
            pltpu.VMEM((rounds, 1, chunk, 128), jnp.float32),
            pltpu.VMEM((rounds, nx, chunk, 128), jnp.float32),
            pltpu.VMEM((rounds, plane * chunk, 128), jnp.float32),
            dma((STEPS, 26)), dma((STEPS, 26)),
            dma((rounds, plane)), dma((rounds, plane)),
            dma((rounds, nx)), dma((rounds, nx)),
            dma((rounds, plane)), dma((rounds, plane)),
        ],
        compiler_params=pltpu.CompilerParams(
            collective_id=0, has_side_effects=True, vmem_limit_bytes=48 * 1024 * 1024
        ),
    )(*args)
    return (
        outs[0].reshape(offsets.shape), outs[1].reshape(charges.shape),
        outs[2].reshape(features.shape), outs[3].reshape(charges.shape),
    )


def solution(mesh):
    grid = P(None, "gx", "gy", "gz", None)
    sizes = tuple(mesh.shape[a] for a in ("gx", "gy", "gz"))
    return jax.shard_map(
        functools.partial(on_device, sizes),
        mesh=mesh,
        in_specs=(grid, grid, grid, P("gx", "gy", "gz")) + (P(),) * 8,
        out_specs=(grid,) * 4,
        check_vma=False,
    )
```

time: 1070 us -> 112 us (0.10)
  waiting for transfers between devices: 414 us -> 0 us
  other arithmetic: 296 us -> 0.78 us
  blocking collectives: 156 us -> 0 us
  matrix products: 138 us -> 0 us
  Pallas kernels: 0 us -> 106 us
  starting transfers between devices: 30.8 us -> 0 us
  between operations: 14.9 us -> 0.7 us
    psum x4 -> x0, waiting for transfers between devices: 409 us -> none  [on_device(): summed = lax.psum(local_rows, ('gx', 'gy', 'gz'))]
    cos x64 -> x0, other arithmetic: 256 us -> none  [phase_table(): return jnp.concatenate([jnp.cos(theta), jnp.sin(theta)], axis=1)]
    psum x4 -> x0, blocking collectives: 156 us -> none  [on_device(): lax.psum((jnp.sum(charge_cells, axis=(0, 2)), jnp.sum(valid_cells)), ('gx...]
    dot_general x130 -> x0, matrix products: 138 us -> none  [the longest x32 55.3 us: field_per_cell(): jnp.dot(weighted, phase_table(frac_rows, wave_float).T, precision=PRECISE)]
    pallas_call x0 -> x1, Pallas kernels: none -> 106 us  [on_device(): pl.pallas_call(functools.partial(kernel_body, sizes, block, chunk), out_s...]
    ppermute x24 -> x0, starting transfers between devices: 30.6 us -> none  [the longest x12 15.9 us: extended(): lax.ppermute(lax.slice_in_dim(block, 0, width, axis=dim), axis, backward)]
    reduce_sum x20 -> x0, other arithmetic: 30.1 us -> none  [the longest x18 28.6 us: pair_messages(): norm_sum = norm_sum + jnp.sum(weight.astype(jnp.float32), axis=-1)]
  transfers between devices with their start and end apart: 28 -> 0, of which waited for: 7 -> 0; matrix products, arithmetic and copies ran while one was open for 27% -> 0% of each run, Pallas kernels for 0% -> 0%
where the time goes in v1:
time: 112 us
  Pallas kernels  106 us (95%)
  local copies, waits for them, and re-layouts  4.38 us (4%)
    pallas_call x1, Pallas kernels, on_device(): pl.pallas_call(functools.partial(kernel_body, sizes, block, chunk), out_s...  106 us
    unnamed x27, local copies, waits for them, and re-layouts  2.98 us

profile of v1, /device:TPU:0, one launch (start us, length us, event | category | flops | bytes accessed | tf_op | source)
XLA Modules:
  0.0 112.0 jit_solution(2933153589641667676)
XLA Ops:
  0.6 0.0 copy-start.10
  0.6 0.0 copy-start.8
  0.7 0.0 copy-start.7
  0.7 0.0 copy-start.9
  0.7 0.0 copy-start.6
  0.7 0.8 compare_convert_fusion
  1.5 0.0 copy-start.4
  1.5 0.0 copy-done.10
  1.5 0.1 copy.17.bias_ref
  1.6 0.0 copy-done.8
  1.6 0.1 copy.19.wmf_ref
  1.6 0.0 copy-done.7
  1.6 0.1 copy.16.wch_ref
  1.7 0.0 copy-done.9
  1.7 0.1 copy.18.wmh_ref
  1.8 0.0 copy-done.6
  1.8 0.0 copy-start.5
  1.8 0.4 copy-done.4
  2.2 0.0 copy-start
  2.2 0.3 copy-done.5
  2.6 0.0 copy-start.1
  2.6 0.0 copy-start.2
  2.6 0.0 copy-start.3
  2.6 0.5 copy-done
  3.1 0.3 copy-done.1
  3.3 0.0 copy-done.2
  3.3 0.0 copy-done.3
  3.3 106.1 %shard_map.147 = (f32[3,1024]{1,0:T(4,128)S(1)}, f32[8,1024]{1,0:T(8,128)S(1)}, bf16[16,1024]{1,0:T(8,128)(2,1)S(1)}, f32[8,1024]{1,0:T(8,128)S(1)}) custom-call(f32[3,1024]{1,0:T(4,128)S(1)} %reshape.61.pos_in, bf16[16,1024]{1,0:T(8,128)(2,1)S(1)} %reshape.62.feat_in, f32[8,1024]{1,0:T(8,128)S(1)} %reshape.63.charge_in, f32[1,1024]{1,0:T(1,128)S(1)} %bitcast.6, ...), custom_call_target="tpu_custom_call" | custom-call | tf_op jit(solution)/shard_map/pallas_call | solution.py:452
  109.5 0.6 reshape.65
  110.1 0.6 copy.20
  110.7 0.6 reshape.67
  111.4 0.6 copy.21
  (3 shorter events, 0.1 us)
Async XLA Ops:
  0.6 0.8 copy-start.10
  0.6 0.9 copy-start.8
  0.7 1.0 copy-start.7
  0.7 1.0 copy-start.9
  0.7 1.1 %copy-start.6 = (f32[3,2,2,2,128]{4,3,2,1,0:T(2,128)S(1)}, f32[3,2,2,2,128]{4,3,2,1,0:T(2,128)}, u32[]{:S(2)}) copy-start(f32[3,2,2,2,128]{4,3,2,1,0:T(2,128)} %param.12) | copy-start | bytes 36868
  1.5 0.8 copy-start.4
  1.8 0.8 copy-start.5
  2.2 0.8 copy-start
  2.6 0.8 copy-start.1
  2.6 0.8 copy-start.2
  2.6 0.8 copy-start.3

commit v2 on v1

--- a/solution.py
+++ b/solution.py
@@ -80,7 +80,7 @@
 
 
 def kernel_body(
-    sizes, block, chunk,
+    sizes, block, chunks,
     pos_in, feat_in, charge_in, valid_in, waves_ref, kern_ref, wfeat_ref, wch_ref, wcf_ref,
     bias_ref, wmh_ref, wmf_ref,
     pos_out, charge_out, feat_out, field_out,
@@ -200,7 +200,7 @@
             rows = [hi, hi, hi, mid, mid, low] + f32(split3(sq - FAR * (1.0 - ok))) + [one]
         return jnp.concatenate(rows + [jnp.zeros((8, width), jnp.float32)], axis=0)
 
-    def pair_messages(step, pos):
+    def pair_prepare(step, pos):
         own = pair_rows(pos + local_f, None, True).astype(jnp.bfloat16)
         for i in range(sx * sy):
             a_ref[i] = own[:, i * sz * CAP : (i + 1) * sz * CAP]
@@ -227,6 +227,7 @@
 
         lax.fori_loop(0, (sx + 2) * (sy + 2), prepare, 0)
 
+    def pair_columns(step, first, last):
         def per_column(i, carry):
             x, y = lax.div(i, sy), lax.rem(i, sy)
             for z in range(sz):
@@ -244,17 +245,20 @@
                 msg_ref[i, :, z * CAP : (z + 1) * CAP] = total
             return carry
 
-        lax.fori_loop(0, sx * sy, per_column, 0)
+        lax.fori_loop(first, last, per_column, 0)
+
+    def pair_finish():
         total = jnp.concatenate([msg_ref[i] for i in range(sx * sy)], axis=1) * valid
         return total[0:16] / jnp.sqrt(jnp.maximum(total[25:26], 1.0))
 
-    def all_sum(r):
+    def sum_scatter(r):
+        rows = chunks[r % ITERS]
         copies = []
         for d in range(1, plane):
             device, p = plane_id(d)
             copy = pltpu.make_async_remote_copy(
-                src_ref=payload.at[r, pl.ds(pl.multiple_of(p * chunk, 8), chunk)],
-                dst_ref=rs_buf.at[r, d],
+                src_ref=payload.at[r, pl.ds(pl.multiple_of(p * rows, 8), rows)],
+                dst_ref=rs_buf.at[r, d, pl.ds(0, rows)],
                 send_sem=rs_send.at[r, d],
                 recv_sem=rs_recv.at[r, d],
                 device_id=device,
@@ -262,16 +266,20 @@
             )
             copy.start()
             copies.append(copy)
-        total = payload[r, pl.ds(pl.multiple_of(mp * chunk, 8), chunk)]
+        return copies
+
+    def sum_across(r, copies):
+        rows = chunks[r % ITERS]
+        total = payload[r, pl.ds(pl.multiple_of(mp * rows, 8), rows)]
         for d in range(1, plane):
             copies[d - 1].wait_recv()
-            total = total + rs_buf[r, d]
-        part_buf[r, 0] = total
+            total = total + rs_buf[r, d, 0:rows]
+        part_buf[r, 0, 0:rows] = total
         copies_x = []
         for d in range(1, nx):
             copy = pltpu.make_async_remote_copy(
-                src_ref=part_buf.at[r, 0],
-                dst_ref=gx_buf.at[r, d],
+                src_ref=part_buf.at[r, 0, pl.ds(0, rows)],
+                dst_ref=gx_buf.at[r, d, pl.ds(0, rows)],
                 send_sem=gx_send.at[r, d],
                 recv_sem=gx_recv.at[r, d],
                 device_id=(lax.rem(mx + d, nx), my, mz),
@@ -279,10 +287,15 @@
             )
             copy.start()
             copies_x.append(copy)
+        return copies_x
+
+    def sum_gather(r, copies_x):
+        rows = chunks[r % ITERS]
+        total = part_buf[r, 0, 0:rows]
         for d in range(1, nx):
             copies_x[d - 1].wait_recv()
-            total = total + gx_buf[r, d]
-        here = pl.ds(pl.multiple_of(mp * chunk, 8), chunk)
+            total = total + gx_buf[r, d, 0:rows]
+        here = pl.ds(pl.multiple_of(mp * rows, 8), rows)
         full[r, here] = total
         copies_g = []
         for d in range(1, plane):
@@ -297,10 +310,26 @@
             )
             copy.start()
             copies_g.append(copy)
+        return copies_g
+
+    def sum_end(copies, copies_x, copies_g):
         for copy in copies_g:
             copy.wait_recv()
         for copy in copies + copies_x + copies_g:
             copy.wait_send()
+
+    def sum_payload(r, charge):
+        qx = jnp.concatenate([x * charge for x in xs], axis=0)
+        qh, ql = split2(qx)
+        payload[r, 0 : N_P * 8] = dot(yh, qh, NT) + (dot(yh, ql, NT) + dot(yl, qh, NT))
+        col = jnp.sum(charge, axis=1, keepdims=True)
+        totals = jnp.sum(jnp.where(lane % 8 == sub, col, 0.0), axis=0, keepdims=True)
+        payload[r, TOT * 8 : TOT * 8 + 8] = jnp.where(sub == 0, totals, count_row)
+        used = (TILES if r % ITERS == 0 else PV0) * 8
+        if plane * chunks[r % ITERS] > used:
+            payload[r, used : plane * chunks[r % ITERS]] = jnp.zeros(
+                (plane * chunks[r % ITERS] - used, 128), jnp.float32
+            )
 
     def trig(pos):
         out = []
@@ -322,7 +351,6 @@
     charge = charge_in[...] * valid
     field = None
     count_row = jnp.zeros((1, 128), jnp.float32) + jnp.sum(valid, axis=1, keepdims=True)
-    ones8 = jnp.ones((8, atoms), jnp.bfloat16)
     for step in range(STEPS):
         copies = send_halo(step, pos, feats)
         (cx, sxn), (cy, syn), (cz, szn) = trig(pos)
@@ -347,9 +375,18 @@
                     n = t * 8 + g
                     packed = jnp.where(lane % 8 == g, pv[n * 8 : n * 8 + 8], packed)
             payload[step * ITERS, (PV0 + t) * 8 : (PV0 + t + 1) * 8] = packed
+        first = step * ITERS
+        sum_payload(first, charge)
+        started = sum_scatter(first)
+        crossed = sum_across(first, started)
         for copy in copies:
             copy.wait()
-        message = pair_messages(step, pos)
+        pair_prepare(step, pos)
+        half = sx * sy // 2
+        pair_columns(step, 0, half)
+        gathered = sum_gather(first, crossed)
+        pair_columns(step, half, sx * sy)
+        message = pair_finish()
         feats = (
             feats.astype(jnp.float32)
             + jnp.tanh(dot(wfeat_ref[...], message, TN, HI))
@@ -357,20 +394,12 @@
         hproj = dot(wch_ref[...], feats.astype(jnp.float32), TN, HI) + bias_ref[...]
         for sweep in range(ITERS):
             r = step * ITERS + sweep
-            qx = jnp.concatenate([x * charge for x in xs], axis=0)
-            qh, ql = split2(qx)
-            payload[r, 0 : N_P * 8] = dot(yh, qh, NT) + (dot(yh, ql, NT) + dot(yl, qh, NT))
-            qrep = jnp.concatenate([charge] * 16, axis=0)
-            th, tm, tl = split3(qrep)
-            totals = dot(ones8, th, NT) + dot(ones8, tm, NT) + dot(ones8, tl, NT)
-            payload[r, TOT * 8 : TOT * 8 + 8] = jnp.where(sub == 0, totals, count_row)
             if sweep > 0:
-                payload[r, PV0 * 8 : TILES * 8] = jnp.zeros((TILES_PV * 8, 128), jnp.float32)
-            if payload.shape[1] > TILES * 8:
-                payload[r, TILES * 8 :] = jnp.zeros(
-                    (payload.shape[1] - TILES * 8, 128), jnp.float32
-                )
-            all_sum(r)
+                sum_payload(r, charge)
+                started = sum_scatter(r)
+                crossed = sum_across(r, started)
+                gathered = sum_gather(r, crossed)
+            sum_end(started, crossed, gathered)
             if sweep == 0:
                 spread = []
                 for n in range(N_P):
@@ -440,6 +469,7 @@
     atoms = sx * sy * sz * CAP
     plane = ny * nz
     chunk = -(-TILES // plane) * 8
+    chunks = (chunk,) + (-(-PV0 // plane) * 8,) * (ITERS - 1)
     rounds = STEPS * ITERS
     valid = (jnp.arange(CAP, dtype=jnp.int32) < counts[..., None]).astype(jnp.float32)
     args = (
@@ -450,7 +480,7 @@
     vmem = pl.BlockSpec(memory_space=pltpu.VMEM)
     dma = pltpu.SemaphoreType.DMA
     outs = pl.pallas_call(
-        functools.partial(kernel_body, sizes, block, chunk),
+        functools.partial(kernel_body, sizes, block, chunks),
         out_shape=(
             jax.ShapeDtypeStruct((3, atoms), jnp.float32),
             jax.ShapeDtypeStruct((8, atoms), jnp.float32),

time: 112 us -> 87.8 us (0.78)
  Pallas kernels: 106 us -> 81.7 us
    pallas_call x1, Pallas kernels: 106 us -> 81.7 us  [on_device(): pl.pallas_call(functools.partial(kernel_body, sizes, block, chunks), out_...]
where the time goes in v2:
time: 87.8 us; the launch traced here: 87.5 us
  Pallas kernels  81.7 us (93%)
  local copies, waits for them, and re-layouts  4.38 us (5%)
    pallas_call x1, Pallas kernels, on_device(): pl.pallas_call(functools.partial(kernel_body, sizes, block, chunks), out_...  81.7 us
    unnamed x27, local copies, waits for them, and re-layouts  2.98 us

profile of v2, /device:TPU:0, one launch (start us, length us, event | category | flops | bytes accessed | tf_op | source)
XLA Modules:
  0.0 87.5 jit_solution(10072084210622294096)
XLA Ops:
  0.6 0.0 copy-start.10
  0.6 0.0 copy-start.8
  0.7 0.0 copy-start.7
  0.7 0.0 copy-start.9
  0.7 0.0 copy-start.6
  0.7 0.8 compare_convert_fusion
  1.5 0.0 copy-start.4
  1.5 0.0 copy-done.10
  1.5 0.1 copy.17.bias_ref
  1.6 0.0 copy-done.8
  1.6 0.1 copy.19.wmf_ref
  1.6 0.0 copy-done.7
  1.6 0.1 copy.16.wch_ref
  1.7 0.0 copy-done.9
  1.7 0.1 copy.18.wmh_ref
  1.8 0.0 copy-done.6
  1.8 0.0 copy-start.5
  1.8 0.4 copy-done.4
  2.2 0.0 copy-start
  2.2 0.3 copy-done.5
  2.6 0.0 copy-start.1
  2.6 0.0 copy-start.2
  2.6 0.0 copy-start.3
  2.6 0.5 copy-done
  3.1 0.3 copy-done.1
  3.3 0.0 copy-done.2
  3.3 0.0 copy-done.3
  3.3 81.7 %shard_map.147 = (f32[3,1024]{1,0:T(4,128)S(1)}, f32[8,1024]{1,0:T(8,128)S(1)}, bf16[16,1024]{1,0:T(8,128)(2,1)S(1)}, f32[8,1024]{1,0:T(8,128)S(1)}) custom-call(f32[3,1024]{1,0:T(4,128)S(1)} %reshape.61.pos_in, bf16[16,1024]{1,0:T(8,128)(2,1)S(1)} %reshape.62.feat_in, f32[8,1024]{1,0:T(8,128)S(1)} %reshape.63.charge_in, f32[1,1024]{1,0:T(1,128)S(1)} %bitcast.6, ...), custom_call_target="tpu_custom_call" | custom-call | tf_op jit(solution)/shard_map/pallas_call | solution.py:482
  85.0 0.6 reshape.65
  85.6 0.6 copy.20
  86.3 0.6 reshape.67
  86.9 0.6 copy.21
  (3 shorter events, 0.1 us)
Async XLA Ops:
  0.6 0.8 copy-start.10
  0.6 0.9 %copy-start.8 = (f32[8,3]{0,1:T(4,128)S(1)}, f32[8,3]{0,1:T(4,128)}, u32[]{:S(2)}) copy-start(f32[8,3]{0,1:T(4,128)} %param.23) | copy-start | bytes 292
  0.7 1.0 %copy-start.7 = (f32[16,8]{0,1:T(8,128)S(1)}, f32[16,8]{0,1:T(8,128)}, u32[]{:S(2)}) copy-start(f32[16,8]{0,1:T(8,128)} %param.19) | copy-start | bytes 1540
  0.7 1.0 %copy-start.9 = (f32[16,3]{0,1:T(4,128)S(1)}, f32[16,3]{0,1:T(4,128)}, u32[]{:S(2)}) copy-start(f32[16,3]{0,1:T(4,128)} %param.22) | copy-start | bytes 580
  0.7 1.1 %copy-start.6 = (f32[3,2,2,2,128]{4,3,2,1,0:T(2,128)S(1)}, f32[3,2,2,2,128]{4,3,2,1,0:T(2,128)}, u32[]{:S(2)}) copy-start(f32[3,2,2,2,128]{4,3,2,1,0:T(2,128)} %param.12) | copy-start | bytes 36868
  1.5 0.8 copy-start.4
  1.8 0.8 copy-start.5
  2.2 0.8 copy-start
  2.6 0.8 copy-start.1
  2.6 0.8 copy-start.2
  2.6 0.8 copy-start.3
